TPU v7x, 32 devices: a whole 2x2x4 slice. The times are simulated.
32 devices in a mesh: seq: 4 (over y, x), ctx: 8 (over z, core).
Axes of the slice: x: 2, y: 2, z: 4, core: 2. Of those that a mesh axis runs over, the one named last changes fastest.
Arguments:
- delta_query: bfloat16 [4, 1024, 2048], P('seq', 'ctx'), may hold values from -6 to 6
- delta_key: bfloat16 [4, 1024, 2048], P('seq', 'ctx'), may hold values from -6 to 6
- delta_value: bfloat16 [4, 1024, 4096], P('seq', 'ctx'), may hold values from -6 to 6
- delta_gate: bfloat16 [4, 1024, 4096], P('seq', 'ctx'), may hold values from -6 to 6
- delta_beta: float32 [4, 32, 1024], P('seq', None, 'ctx'), may hold values from 0 to 1
- delta_decay: float32 [4, 32, 1024], P('seq', None, 'ctx'), may hold values from -2 to 0
- norm_gain: float32 [128], replicated, may hold values from 0.5 to 1.5
- attention_query: bfloat16 [4, 1024, 4096], P('seq', 'ctx'), may hold values from -4 to 4
- attention_key_value: bfloat16 [4, 1024, 1024], P('seq', 'ctx'), may hold values from -4 to 4
- attention_gate: bfloat16 [4, 1024, 4096], P('seq', 'ctx'), may hold values from -6 to 6
- moe_input: bfloat16 [4, 1024, 2048], P('seq', 'ctx'), may hold values from -6 to 6
- routes: int32 [4, 1024, 10], P('seq', 'ctx'), may hold values from 0 to 31, all different within a row; in each aligned block of 128 rows (0 to 127, 128 to 255, ..., all dimensions but the last counted through in order) at most 64 rows name the same one
- drop_mask: int32 [4, 1024, 10], P('seq', 'ctx'), may hold values 0 or 1
- route_weights: float32 [4, 1024, 10], P('seq', 'ctx'), may hold values from 0.05 to 0.5
- w_gate: bfloat16 [32, 2048, 512], P(('seq', 'ctx')), may hold values from -0.125 to 0.125
- w_up: bfloat16 [32, 2048, 512], P(('seq', 'ctx')), may hold values from -0.125 to 0.125
- w_down: bfloat16 [32, 512, 2048], P(('seq', 'ctx')), may hold values from -0.25 to 0.25
Outputs:
- delta_out: bfloat16 [4, 1024, 4096], P('seq', 'ctx')
- attn_out: bfloat16 [4, 1024, 4096], P('seq', 'ctx')
- moe_out: bfloat16 [4, 1024, 2048], P('seq', 'ctx')
Inputs may be any that keep to these rules, and one draw needn't show every extreme that they name: `routes`: within the rows of one device (aligned blocks of 128 positions), each token names 10 different experts and no expert is named more than 64 times; in some block some expert is named exactly 64 times. `drop_mask`: 1 keeps the chosen expert, 0 drops it.
All inputs are finite; a program needn't handle non-finite values. No bound on the sum of `drop_mask` on one device may be relied on, other than what follows from the above.
Results may differ from a plain program's by a relative error of at most 0.011.
Values may be sent and summed in bfloat16 or wider, within the bound.
A program may use at most 384 MiB of HBM per device.

v0:
```python
import math

import jax
import jax.numpy as jnp
from jax import lax
from jax.sharding import PartitionSpec as P

HV = 32
HKD = 16
DK = 128
DV = 128
QUERY_HEADS = 16
KEY_VALUE_HEADS = 2
HEAD_WIDTH = 256
SPAN = 64


precise = lax.Precision.HIGHEST


def prefix(x, axis, combine, identity):
    length, index = (lax.axis_size(axis), lax.axis_index(axis))
    everything = jax.tree.map(lambda part: lax.all_gather(part, axis), x)
    start = jax.tree.map(
        lambda part, zero: jnp.broadcast_to(jnp.asarray(zero, part.dtype), part.shape), x, identity
    )

    def lap(k, before):
        reached = k < index
        new = combine(before, jax.tree.map(lambda part: part[k], everything))
        return jax.tree.map(lambda a, b: jnp.where(reached, a, b), new, before)

    return lax.fori_loop(0, length, lap, start)


def shifted(block, axis, distance):
    devices = range(lax.axis_size(axis))
    route = [(i - distance, i) for i in devices if i - distance in devices]
    return lax.ppermute(block, axis, route)


def unit_rows(matrix):
    return matrix / jnp.sqrt(jnp.sum(matrix * matrix, axis=-1, keepdims=True) + 1e-06)


def span_terms(query_rows, keys, value_rows, beta, decay):
    size = decay.shape[-1]
    key_dim = keys.shape[-1]
    value_dim = value_rows.shape[-1]
    cumulative = jnp.cumsum(decay, axis=-1)
    place_list = jnp.arange(size)
    lower = place_list[:, None] >= place_list[None, :]
    strict = place_list[:, None] > place_list[None, :]
    spread = cumulative[..., :, None] - cumulative[..., None, :]
    decay_ratio = jnp.exp(jnp.where(lower, spread, -1e30))
    key_key = jnp.einsum("...ik,...jk->...ij", keys, keys, precision=precise)
    query_key = jnp.einsum("...ik,...jk->...ij", query_rows, keys, precision=precise)
    system = jnp.eye(size, dtype=jnp.float32) + jnp.where(
        strict, beta[..., :, None] * decay_ratio * key_key, 0.0
    )
    retained = jnp.exp(cumulative)
    right_side = jnp.concatenate(
        [beta[..., None] * value_rows, (beta * retained)[..., None] * keys], axis=-1
    )
    solved = jax.scipy.linalg.solve_triangular(system, right_side, lower=True, unit_diagonal=True)
    new_values = solved[..., :value_dim]
    new_keys = solved[..., value_dim:]
    mixing = decay_ratio * query_key
    query_eff = retained[..., None] * query_rows - jnp.einsum(
        "...ij,...jk->...ik", mixing, new_keys, precision=precise
    )
    direct = jnp.einsum("...ij,...jv->...iv", mixing, new_values, precision=precise)
    tail_keys = jnp.exp(cumulative[..., -1:] - cumulative)[..., None] * keys
    carry_a = retained[..., -1:, None] * jnp.eye(key_dim, dtype=jnp.float32) - jnp.einsum(
        "...ck,...cl->...kl", new_keys, tail_keys, precision=precise
    )
    carry_b = jnp.einsum("...cv,...cl->...vl", new_values, tail_keys, precision=precise)
    return (query_eff, direct, carry_a, carry_b)


def compose(earlier, later):
    joined_a = jnp.einsum("hij,hjk->hik", earlier[0], later[0], precision=precise)
    joined_b = jnp.einsum("hvk,hkl->hvl", earlier[1], later[0], precision=precise) + later[1]
    return (joined_a, joined_b)


def gated_norm(outputs, delta_gate, norm_gain):
    scale = lax.rsqrt(jnp.mean(outputs * outputs, axis=-1, keepdims=True) + 1e-06)
    gate_vals = delta_gate.astype(jnp.float32).reshape(outputs.shape)
    normed = outputs * scale * norm_gain * jax.nn.silu(gate_vals)
    return normed.astype(jnp.bfloat16).reshape(delta_gate.shape)


def delta_mixer(
    delta_query, delta_key, delta_value, delta_gate, delta_beta, delta_decay, norm_gain
):
    token_count = delta_query.shape[1]
    n_spans = token_count // SPAN
    head_repeat = HV // HKD
    query_rows = unit_rows(delta_query[0].astype(jnp.float32).reshape(token_count, HKD, DK)) * (
        1.0 / math.sqrt(DK)
    )
    query_rows = jnp.repeat(query_rows, head_repeat, axis=1)
    keys = jnp.repeat(
        unit_rows(delta_key[0].astype(jnp.float32).reshape(token_count, HKD, DK)),
        head_repeat,
        axis=1,
    )
    value_rows = delta_value[0].astype(jnp.float32).reshape(token_count, HV, DV)

    def to_spans(array):
        return array.reshape(n_spans, SPAN, HV, array.shape[-1]).transpose(2, 0, 1, 3)

    query_eff, direct, carry_a, carry_b = span_terms(
        to_spans(query_rows),
        to_spans(keys),
        to_spans(value_rows),
        delta_beta[0].reshape(HV, n_spans, SPAN),
        delta_decay[0].reshape(HV, n_spans, SPAN),
    )
    identity = jnp.broadcast_to(jnp.eye(DK, dtype=jnp.float32), (HV, DK, DK))
    zero_state = jnp.zeros((HV, DV, DK), jnp.float32)
    starts_a = [identity]
    starts_b = [zero_state]
    for span_id in range(n_spans):
        starts_a.append(
            jnp.einsum("hij,hjk->hik", starts_a[-1], carry_a[:, span_id], precision=precise)
        )
        starts_b.append(
            jnp.einsum("hvk,hkl->hvl", starts_b[-1], carry_a[:, span_id], precision=precise)
            + carry_b[:, span_id]
        )
    incoming = prefix((starts_a[-1], starts_b[-1]), "ctx", compose, (identity, zero_state))
    state_in = incoming[1]
    before_a = jnp.stack(starts_a[:-1], axis=1)
    before_b = jnp.stack(starts_b[:-1], axis=1)
    states = jnp.einsum("hvk,hckl->hcvl", state_in, before_a, precision=precise) + before_b
    outputs = jnp.einsum("hcik,hcvk->hciv", query_eff, states, precision=precise) + direct
    outputs = outputs.transpose(1, 2, 0, 3).reshape(token_count, HV, DV)
    return gated_norm(outputs, delta_gate, norm_gain)


def window_attention(attention_query, window_key_value, attention_gate, base):
    local_sequences = attention_query.shape[0]
    token_count = attention_query.shape[1]
    head_groups = QUERY_HEADS // KEY_VALUE_HEADS
    query_rows = attention_query.reshape(
        local_sequences, token_count, KEY_VALUE_HEADS, head_groups, HEAD_WIDTH
    )
    key_value = window_key_value.reshape(
        local_sequences, 2 * token_count, 2, KEY_VALUE_HEADS, HEAD_WIDTH
    )
    scores = jnp.einsum(
        "stkgd,sukd->skgtu", query_rows, key_value[:, :, 0], preferred_element_type=jnp.float32
    ) * (1.0 / math.sqrt(HEAD_WIDTH))
    query_pos = base + jnp.arange(token_count, dtype=jnp.int32)
    key_pos = base - token_count + jnp.arange(2 * token_count, dtype=jnp.int32)
    visible = (
        (key_pos[None, :] <= query_pos[:, None])
        & (key_pos[None, :] > query_pos[:, None] - token_count)
        & (key_pos[None, :] >= 0)
    )
    scores = jnp.where(visible, scores, -jnp.inf)
    row_max = jnp.max(scores, axis=-1, keepdims=True)
    lifted = jnp.exp(scores - row_max)
    probs = (lifted / jnp.sum(lifted, axis=-1, keepdims=True)).astype(jnp.bfloat16)
    mixed = jnp.einsum(
        "skgtu,sukd->stkgd", probs, key_value[:, :, 1], preferred_element_type=jnp.float32
    )
    gated = mixed * jax.nn.sigmoid(attention_gate.astype(jnp.float32).reshape(mixed.shape))
    return gated.astype(jnp.bfloat16).reshape(attention_query.shape)


def slot_numbers(expert_ids, experts):
    row_count = expert_ids.shape[0]
    onehot = (expert_ids[:, None] == jnp.arange(experts, dtype=jnp.int32)[None, :]).astype(
        jnp.bfloat16
    )
    place_list = jnp.arange(row_count, dtype=jnp.int32)
    before = (place_list[:, None] > place_list[None, :]).astype(jnp.bfloat16)
    earlier = jnp.dot(before, onehot, preferred_element_type=jnp.float32)
    return jnp.sum(earlier * onehot.astype(jnp.float32), axis=1).astype(jnp.int32)


def expert_layer(moe_input, routes, drop_mask, route_weights, w_gate, w_up, w_down):
    token_count = moe_input.shape[1]
    width = moe_input.shape[2]
    top_count = routes.shape[2]
    n_seq = lax.axis_size("seq")
    n_ctx = lax.axis_size("ctx")
    n_dev = n_seq * n_ctx
    capacity = max(2, token_count * top_count * 8 // (n_dev * 5))
    expert_ids = routes[0].reshape(-1)
    keep_flags = drop_mask[0].reshape(-1)
    target = expert_ids * capacity + slot_numbers(expert_ids, n_dev)
    rows = jnp.repeat(moe_input[0], top_count, axis=0) * keep_flags[:, None].astype(jnp.bfloat16)
    outgoing = jnp.zeros((n_dev * capacity, width), jnp.bfloat16).at[target].set(rows)
    arrived = lax.all_to_all(
        outgoing.reshape(n_dev, capacity, width),
        ("seq", "ctx"),
        split_axis=0,
        concat_axis=0,
        tiled=True,
    )
    flat_rows = arrived.reshape(-1, width)
    gate_part = jnp.dot(flat_rows, w_gate[0], preferred_element_type=jnp.float32)
    up_part = jnp.dot(flat_rows, w_up[0], preferred_element_type=jnp.float32)
    hidden = (jax.nn.silu(gate_part) * up_part).astype(jnp.bfloat16)
    result = jnp.dot(hidden, w_down[0], preferred_element_type=jnp.float32).astype(jnp.bfloat16)
    returned = lax.all_to_all(
        result.reshape(arrived.shape), ("seq", "ctx"), split_axis=0, concat_axis=0, tiled=True
    )
    results = returned.reshape(n_dev * capacity, width)[target]
    weights = keep_flags.astype(jnp.float32) * route_weights[0].reshape(-1)
    combined = jnp.einsum(
        "tkd,tk->td",
        results.reshape(token_count, top_count, width).astype(jnp.float32),
        weights.reshape(token_count, top_count),
    )
    return combined.astype(jnp.bfloat16)[None]


def body(
    delta_query,
    delta_key,
    delta_value,
    delta_gate,
    delta_beta,
    delta_decay,
    norm_gain,
    attention_query,
    attention_key_value,
    attention_gate,
    moe_input,
    routes,
    drop_mask,
    route_weights,
    w_gate,
    w_up,
    w_down,
):
    delta_out = delta_mixer(
        delta_query, delta_key, delta_value, delta_gate, delta_beta, delta_decay, norm_gain
    )
    previous = shifted(attention_key_value, "ctx", 1)
    window_key_value = jnp.concatenate([previous, attention_key_value], axis=1)
    base = lax.axis_index("ctx") * attention_query.shape[1]
    attn_out = window_attention(attention_query, window_key_value, attention_gate, base)
    moe_out = expert_layer(moe_input, routes, drop_mask, route_weights, w_gate, w_up, w_down)
    return (delta_out, attn_out, moe_out)


def solution(mesh):
    placed = (
        P("seq", "ctx", None),
        P("seq", "ctx", None),
        P("seq", "ctx", None),
        P("seq", "ctx", None),
        P("seq", None, "ctx"),
        P("seq", None, "ctx"),
        P(),
        P("seq", "ctx", None),
        P("seq", "ctx", None),
        P("seq", "ctx", None),
        P("seq", "ctx", None),
        P("seq", "ctx", None),
        P("seq", "ctx", None),
        P("seq", "ctx", None),
        P(("seq", "ctx"), None, None),
        P(("seq", "ctx"), None, None),
        P(("seq", "ctx"), None, None),
    )
    return jax.shard_map(
        body,
        mesh=mesh,
        in_specs=placed,
        out_specs=(P("seq", "ctx", None), P("seq", "ctx", None), P("seq", "ctx", None)),
        check_vma=False,
    )
```

profile of v0, /device:TPU:18, one launch (start us, length us, event | category | flops | bytes accessed | tf_op | source)
XLA Modules:
  0.0 1047.9 jit_solution(14906747426432124566)
XLA Ops:
  17.1 4.8 fusion.87
  30.1 4.8 fusion.86
  38.8 10.2 add_bitcast_fusion
  49.0 134.2 %custom-call.4 = f32[32,2,1,64,64]{0,3,4,2,1:T(8,128)} custom-call(f32[32,2,1,64,64]{0,4,3,2,1:T(8,128)} %get-tuple-element.150), custom_call_target="InvertDiagBlocksLowerTriangular" | custom-call | tf_op jit(solution)/shard_map/jit(_solve_triangular)/vmap(vmap())/triangular_solve | solution.py:65
  183.3 5.3 copy.90
  195.3 8.2 multiply_subtract_fusion
  212.6 4.4 broadcast_in_dim.82
  217.0 10.3 reshape.287
  227.3 20.1 %scatter_custom_fusion = bf16[2048,2048]{1,0:T(8,128)(2,1)} fusion(s32[1280]{0:T(1024)S(1)} %fusion.80, bf16[1280,2048]{1,0:T(8,128)(2,1)} %reshape.287, bf16[]{:T(256)} %constant.73.clone.1, bf16[1280]{0:T(1024)(128)(2,1)S(1)} %convert_element_type.125), kind=kCustom, calls=%fused_computation.16 | custom fusion | flops 2621440 | bytes 13635586 | tf_op jit(solution)/shard_map/scatter | solution.py:197
  247.4 5.9 all-to-all-start
  253.4 9.6 fusion.53
  269.7 334.0 %all-to-all-done = bf16[32,64,2048]{2,1,0:T(8,128)(2,1)} async-done(((bf16[32,64,2048]{2,1,0:T(8,128)(2,1)}), bf16[32,64,2048]{2,1,0:T(8,128)(2,1)}, u32[]{:S(2)}, u32[]{:S(2)}) %all-to-all-start) | async-done | bytes 8388640 | tf_op jit(solution)/shard_map/all_to_all | solution.py:198
  603.8 7.7 fusion.41
  611.5 9.3 multiply_convert_fusion
  620.8 6.8 convolution_convert_fusion
  627.5 8.5 all-to-all-start.1
  644.2 5.3 fusion.51
  659.5 195.5 %collective-permute-done = bf16[1,128,1024]{1,2,0:T(8,128)(2,1)} collective-permute-done((bf16[1,128,1024]{1,2,0:T(8,128)(2,1)S(1)}, bf16[1,128,1024]{1,2,0:T(8,128)(2,1)}, u32[]{:S(2)}, u32[]{:S(2)}) %collective-permute-start) | collective-permute-done | bytes 262176 | tf_op jit(solution)/shard_map/ppermute | solution.py:39
  859.7 118.3 %while.14 = (s32[]{:T(128)}, f32[32,128,128]{1,2,0:T(8,128)}, s32[]{:T(128)}, f32[8,32,128,128]{3,2,1,0:T(8,128)}, f32[8,32,128,128]{3,2,1,0:T(8,128)}, /*index=5*/s32[]{:T(128)}, s32[]{:T(128)}) while((s32[]{:T(128)}, f32[32,128,128]{1,2,0:T(8,128)}, s32[]{:T(128)}, f32[8,32,128,128]{3,2,1,0:T(8,128)}, ...), condition=%wide.region_4.5_spmd.clone, body=%wide.region_3.4_spmd.clone.sunk | while | flops 807403520 | bytes 23070828 | solution.py:33
  867.5 7.1 fusion.108
  882.3 7.1 fusion.108
  897.1 7.1 fusion.108
  911.8 7.1 fusion.108
  926.6 7.1 fusion.108
  941.3 7.1 fusion.108
  956.1 7.1 fusion.108
  970.9 7.1 fusion.108
  979.5 6.7 bitcast_add_fusion.1
  986.2 9.4 multiply_reduce_fusion
  1009.9 15.3 %gather_fusion = bf16[1280,2048]{1,0:T(8,128)(2,1)} fusion(bf16[2048,2048]{1,0:T(8,128)(2,1)} %bitcast.44, s32[2048]{0:T(1024)S(1)} %copy-done.31), kind=kCustom, calls=%fused_computation | custom fusion | bytes 10490880 | tf_op jit(solution)/shard_map/gather | solution.py:213
  1025.2 9.6 reshape.292
  1034.8 4.9 fusion.88
  (193 shorter events, 145.7 us)
Async XLA Ops:
  7.2 613.6 %copy-start = (bf16[1,512,2048]{2,1,0:T(8,128)(2,1)S(1)}, bf16[1,512,2048]{2,1,0:T(8,128)(2,1)}, u32[]{:S(2)}) copy-start(bf16[1,512,2048]{2,1,0:T(8,128)(2,1)} %param.35) | copy-start | bytes 6291460
  7.2 852.5 %all-gather.5.cloned.1.call-start = ((), (), s32[]{:S(2)}) async-start(), calls=%async_computation.2 | async-start | bytes 18874368 | tf_op jit(solution)/shard_map/all_gather | solution.py:23
  17.1 4.8 copy-start.2
  17.1 4.8 copy-start.29
  27.7 2.3 copy-start.3
  34.9 3.9 copy-start.28
  34.9 3.9 copy-start.30
  34.9 3.9 copy-start.32
  34.9 3.9 copy-start.33
  183.3 5.3 copy-start.19
  191.4 3.9 copy-start.4
  195.3 8.2 copy-start.6
  247.4 356.3 %all-to-all-start = ((bf16[32,64,2048]{2,1,0:T(8,128)(2,1)}), bf16[32,64,2048]{2,1,0:T(8,128)(2,1)}, u32[]{:S(2)}, u32[]{:S(2)}) async-start(bf16[32,64,2048]{2,1,0:T(8,128)(2,1)} %bitcast.163), calls=%async_computation | async-start | bytes 16777216 | tf_op jit(solution)/shard_map/all_to_all | solution.py:198
  253.3 606.4 %all-gather.7.cloned.1.call-start = ((), (), s32[]{:S(2)}) async-start(), calls=%async_computation.3 | async-start | bytes 18874368 | tf_op jit(solution)/shard_map/all_gather | solution.py:23
  253.3 9.6 copy-start.9
  603.8 7.7 copy-start.38
  627.5 8.5 copy-start.26
  627.5 382.4 %all-to-all-start.1 = ((bf16[32,64,2048]{2,1,0:T(8,128)(2,1)}), bf16[32,64,2048]{2,1,0:T(8,128)(2,1)}, u32[]{:S(2)}, u32[]{:S(2)}) async-start(bf16[32,64,2048]{2,1,0:T(8,128)(2,1)} %bitcast.170), calls=%async_computation.1 | async-start | bytes 16777216 | tf_op jit(solution)/shard_map/all_to_all | solution.py:210
  636.2 218.9 %collective-permute-start = (bf16[1,128,1024]{1,2,0:T(8,128)(2,1)S(1)}, bf16[1,128,1024]{1,2,0:T(8,128)(2,1)}, u32[]{:S(2)}, u32[]{:S(2)}) collective-permute-start(bf16[1,128,1024]{1,2,0:T(8,128)(2,1)S(1)} %copy.104), channel_id=1, source_target_pairs={{0,1},{1,2},{2,3},{3,4},{4,5},{5,6},{6,7},{8,9},{9,10},{10,11},{11... | collective-permute-start | bytes 786440 | tf_op jit(solution)/shard_map/ppermute | solution.py:39
  638.2 5.4 copy-start.36
  638.2 5.9 copy-start.37
  644.2 5.3 copy-start.7
  649.5 3.6 copy-start.20
  653.1 2.5 copy-start.21
  656.8 199.2 %copy-start.22 = (bf16[16,8,16,256]{3,2,1,0:T(8,128)(2,1)S(1)}, bf16[16,8,16,256]{3,2,1,0:T(8,128)(2,1)}, u32[]{:S(2)}) copy-start(bf16[16,8,16,256]{3,2,1,0:T(8,128)(2,1)} %copy.134) | copy-start | bytes 3145732
  979.5 6.7 copy-start.11
  979.5 6.7 copy-start.16
  979.5 6.7 copy-start.17
  979.5 6.7 copy-start.27
  1003.8 2.8 copy-start.23
  1006.7 3.3 copy-start.31
  1034.8 6.0 copy-start.1
  (12 other events, 17.9 us)
Sparse Core Ops, SparseCore 0:
  210.5 290.2 all-gather.4
  502.4 270.5 all-gather.6
where the time goes:
time: 1060 us; the launch traced here: 1050 us
  waiting for transfers between devices  530 us (50%)
  other arithmetic  182 us (17%)
  matrix products  155 us (15%)
  local copies, waits for them, and re-layouts  150 us (14%)
  starting transfers between devices  16.4 us (2%)
  between operations  14.9 us (1%)
    all_to_all x1, waiting for transfers between devices, expert_layer(): lax.all_to_all(outgoing.reshape(n_dev, capacity, width), ('seq', 'ctx'),...  334 us
    ppermute x1, waiting for transfers between devices, shifted(): return lax.ppermute(block, axis, route)  196 us
    another operation x4, other arithmetic, span_terms(): jax.scipy.linalg.solve_triangular(system, right_side, lower=True, unit_di...  145 us
    dot_general x8, matrix products, compose(): jnp.einsum('hvk,hkl->hvl', earlier[1], later[0], precision=precise)  56.5 us
    dynamic_slice x16, local copies, waits for them, and re-layouts, lap(): new = combine(before, jax.tree.map(lambda part: part[k], everything))  48.9 us
  transfers between devices with their start and end apart: 5, of which 2 were waited for; matrix products, arithmetic and copies ran while one was open for 24% of the time, Pallas kernels for 0%

commit v1 on v0

v1 whole, which is shorter than its diff:
```python
import functools
import math

import jax
import jax.numpy as jnp
from jax import lax
from jax.experimental import pallas as pl
from jax.experimental.pallas import tpu as pltpu
from jax.sharding import PartitionSpec as P

HV = 32
HKD = 16
DK = 128
DV = 128
QUERY_HEADS = 16
KEY_VALUE_HEADS = 2
HEAD_WIDTH = 256
PACK = DV + DK + 16
F32 = jnp.float32
BF16 = jnp.bfloat16
VMEM = 50 * 1024 * 1024


def halves(a):
    high = a.astype(BF16)
    return high, (a - high.astype(F32)).astype(BF16)


def mm(a, b):
    return jnp.dot(a, b, preferred_element_type=F32)


def mm_nt(a, b):
    return lax.dot_general(a, b, (((1,), (1,)), ((), ())), preferred_element_type=F32)


def mm_tn(a, b):
    return lax.dot_general(a, b, (((0,), (0,)), ((), ())), preferred_element_type=F32)


def mm_square(a, b):
    a_high, a_low = halves(a)
    b_high, b_low = halves(b)
    row = jnp.concatenate([b_high, b_low], axis=1)
    both = mm(jnp.concatenate([a_high, a_low], axis=1), jnp.concatenate([row, row], axis=0))
    width = b.shape[1]
    return both[:, :width] + both[:, width:]


def column(row, size):
    return jnp.broadcast_to(row, (size, row.shape[1])).T


def unit_scale(rows):
    return 1.0 / jnp.sqrt(jnp.sum(rows * rows, axis=-1, keepdims=True) + 1e-06)


def delta_local_kernel(key_heads, q_ref, k_ref, v_ref, beta_ref, cum_ref, eff_ref, direct_ref, pack_ref):
    size = q_ref.shape[0]
    repeat = HV // HKD
    row_id = lax.broadcasted_iota(jnp.int32, (size, size), 0)
    col_id = lax.broadcasted_iota(jnp.int32, (size, size), 1)
    lower = row_id >= col_id
    strict = row_id > col_id
    keys, key_key, query_key, query_rows, key_cols, key_rows = [], [], [], [], [], []
    for a in range(key_heads):
        kb = k_ref[:, a * DK : (a + 1) * DK]
        qb = q_ref[:, a * DK : (a + 1) * DK]
        kf, qf = kb.astype(F32), qb.astype(F32)
        k_col = unit_scale(kf)
        q_col = unit_scale(qf) * (1.0 / math.sqrt(DK))
        k_row = jnp.broadcast_to(k_col, (size, size)).T
        keys.append(kb)
        key_cols.append(k_col)
        key_rows.append(k_row[:1])
        query_rows.append(qf * q_col)
        key_key.append(mm_nt(kb, kb) * k_col * k_row)
        query_key.append(mm_nt(qb, kb) * q_col * k_row)
    heads = range(key_heads * repeat)
    ratio, near, inverse, cum_cols = [], [], [], []
    for h in heads:
        cum = cum_ref[h : h + 1, :]
        cum_col = column(cum, size)
        spread = jnp.exp(jnp.where(lower, cum_col - cum, -1e30))
        n = jnp.where(strict, column(beta_ref[h : h + 1, :], size) * spread * key_key[h // repeat], 0.0)
        ratio.append(spread)
        near.append(n)
        cum_cols.append(cum_col)
        first = (row_id // 2) == (col_id // 2)
        inverse.append(jnp.where(row_id == col_id, 1.0, jnp.where(first, -n, 0.0)))
    span = 2
    while span < size:
        part = (row_id // (2 * span) == col_id // (2 * span)) & (row_id // span > col_id // span)
        inner = [mm_square(jnp.where(part, near[h], 0.0), inverse[h]) for h in heads]
        inverse = [inverse[h] - mm_square(inverse[h], inner[h]) for h in heads]
        span *= 2
    for h in heads:
        a = h // repeat
        kb = keys[a]
        cum = cum_ref[h : h + 1, :]
        beta = beta_ref[h : h + 1, :]
        vb = v_ref[:, h * DV : (h + 1) * DV]
        left_v = jnp.concatenate(halves(inverse[h] * beta), axis=1)
        left_k = jnp.concatenate(halves(inverse[h] * (beta * jnp.exp(cum) * key_rows[a])), axis=1)
        solved = jnp.concatenate(
            [
                mm(left_v, jnp.concatenate([vb, vb], axis=0)),
                mm(left_k, jnp.concatenate([kb, kb], axis=0)),
            ],
            axis=1,
        )
        mix_high, mix_low = halves(ratio[h] * query_key[a])
        solved_high, solved_low = halves(solved)
        mixed = mm(
            jnp.concatenate([mix_high, mix_low], axis=1),
            jnp.concatenate([solved_high, solved_high], axis=0),
        ) + mm(mix_high, solved_low)
        direct_ref[h] = mixed[:, :DV]
        cum_col = cum_cols[h][:, :1]
        eff_ref[h] = jnp.exp(cum_col) * query_rows[a] - mixed[:, DV:]
        last = cum[:, size - 1 : size]
        tail = solved * (jnp.exp(last - cum_col) * key_cols[a])
        tail_high, tail_low = halves(tail)
        carry = mm_tn(
            jnp.concatenate([tail_high, tail_low], axis=0), jnp.concatenate([kb, kb], axis=0)
        )
        pack_ref[h, : DV + DK, :] = carry.astype(BF16)
        kept = jnp.broadcast_to(jnp.exp(last), (8, DK))
        kept_high = kept.astype(BF16).astype(F32)
        pack_ref[h, DV + DK :, :] = jnp.concatenate([kept_high, kept - kept_high], axis=0).astype(BF16)


def delta_local(delta_query, delta_key, delta_value, beta, cumulative):
    size = delta_query.shape[0]
    key_heads = 4
    heads = key_heads * (HV // HKD)
    return pl.pallas_call(
        functools.partial(delta_local_kernel, key_heads),
        grid=(HKD // key_heads,),
        in_specs=[
            pl.BlockSpec((size, key_heads * DK), lambda i: (0, i)),
            pl.BlockSpec((size, key_heads * DK), lambda i: (0, i)),
            pl.BlockSpec((size, heads * DV), lambda i: (0, i)),
            pl.BlockSpec((heads, size), lambda i: (i, 0)),
            pl.BlockSpec((heads, size), lambda i: (i, 0)),
        ],
        out_specs=[
            pl.BlockSpec((heads, size, DK), lambda i: (i, 0, 0)),
            pl.BlockSpec((heads, size, DV), lambda i: (i, 0, 0)),
            pl.BlockSpec((heads, PACK, DK), lambda i: (i, 0, 0)),
        ],
        out_shape=[
            jax.ShapeDtypeStruct((HV, size, DK), F32),
            jax.ShapeDtypeStruct((HV, size, DV), F32),
            jax.ShapeDtypeStruct((HV, PACK, DK), BF16),
        ],
        compiler_params=pltpu.CompilerParams(vmem_limit_bytes=VMEM),
        cost_estimate=pl.CostEstimate(
            flops=60_000_000_000, bytes_accessed=12_000_000, transcendentals=1_000_000
        ),
        name="delta_local",
    )(delta_query, delta_key, delta_value, beta, cumulative)


def delta_finish_kernel(heads, pack_ref, eff_ref, direct_ref, gate_ref, gain_ref, out_ref, state_ref):
    index = lax.axis_index("ctx")
    state_ref[...] = jnp.zeros_like(state_ref)

    def lap(k, unused):
        for h in range(heads):
            state = state_ref[h]
            new = pack_ref[k, h, :DV, :].astype(F32)
            change = pack_ref[k, h, DV : DV + DK, :]
            kept = pack_ref[k, h, DV + DK :, :].astype(F32)
            kept = kept[:1] + kept[8:9]
            moved = mm(
                jnp.concatenate(halves(state), axis=1), jnp.concatenate([change, change], axis=0)
            )
            state_ref[h] = kept * state - moved + new
        return unused

    lax.fori_loop(0, index, lap, 0)
    for h in range(heads):
        state_high, state_low = halves(state_ref[h])
        eff_high, eff_low = halves(eff_ref[h])
        rows = (
            mm_nt(
                jnp.concatenate([eff_high, eff_low], axis=1),
                jnp.concatenate([state_high, state_high], axis=1),
            )
            + mm_nt(eff_high, state_low)
            + direct_ref[h]
        )
        scale = lax.rsqrt(jnp.mean(rows * rows, axis=-1, keepdims=True) + 1e-06)
        gate = gate_ref[:, h * DV : (h + 1) * DV].astype(F32)
        gated = rows * scale * gain_ref[...] * (gate / (1.0 + jnp.exp(-gate)))
        out_ref[:, h * DV : (h + 1) * DV] = gated.astype(BF16)


def delta_finish(packs, eff, direct, gate, gain):
    size = gate.shape[0]
    heads = 4
    count = packs.shape[0]
    return pl.pallas_call(
        functools.partial(delta_finish_kernel, heads),
        grid=(HV // heads,),
        in_specs=[
            pl.BlockSpec((count, heads, PACK, DK), lambda i: (0, i, 0, 0)),
            pl.BlockSpec((heads, size, DK), lambda i: (i, 0, 0)),
            pl.BlockSpec((heads, size, DV), lambda i: (i, 0, 0)),
            pl.BlockSpec((size, heads * DV), lambda i: (0, i)),
            pl.BlockSpec((1, DV), lambda i: (0, 0)),
        ],
        out_specs=pl.BlockSpec((size, heads * DV), lambda i: (0, i)),
        out_shape=jax.ShapeDtypeStruct((size, HV * DV), BF16),
        scratch_shapes=[pltpu.VMEM((heads, DV, DK), F32)],
        compiler_params=pltpu.CompilerParams(vmem_limit_bytes=VMEM),
        cost_estimate=pl.CostEstimate(
            flops=20_000_000_000, bytes_accessed=24_000_000, transcendentals=1_000_000
        ),
        name="delta_finish",
    )(packs, eff, direct, gate, gain)


def attention_kernel(heads, q_ref, k_old_ref, v_old_ref, k_ref, v_ref, gate_ref, out_ref):
    size = q_ref.shape[0]
    row_id = lax.broadcasted_iota(jnp.int32, (size, size), 0)
    col_id = lax.broadcasted_iota(jnp.int32, (size, size), 1)
    first = jnp.where(lax.axis_index("ctx") > 0, 0, size)
    seen_old = col_id > row_id + first
    seen = col_id <= row_id
    k_all = jnp.concatenate([k_old_ref[...], k_ref[...]], axis=0)
    v_all = jnp.concatenate([v_old_ref[...], v_ref[...]], axis=0)
    visible = jnp.concatenate([seen_old, seen], axis=1)
    for h in range(heads):
        part = slice(h * HEAD_WIDTH, (h + 1) * HEAD_WIDTH)
        scores = mm_nt(q_ref[:, part], k_all) * (1.0 / math.sqrt(HEAD_WIDTH))
        scores = jnp.where(visible, scores, -jnp.inf)
        lifted = jnp.exp(scores - jnp.max(scores, axis=-1, keepdims=True))
        probs = (lifted / jnp.sum(lifted, axis=-1, keepdims=True)).astype(BF16)
        gate = gate_ref[:, part].astype(F32)
        out_ref[:, part] = (mm(probs, v_all) / (1.0 + jnp.exp(-gate))).astype(BF16)


def window_attention(query, previous, key_value, gate):
    size = query.shape[0]
    heads = 4
    per_group = QUERY_HEADS // KEY_VALUE_HEADS // heads
    wide = pl.BlockSpec((size, heads * HEAD_WIDTH), lambda i: (0, i))
    key = pl.BlockSpec((size, HEAD_WIDTH), lambda i: (0, i // per_group))
    value = pl.BlockSpec((size, HEAD_WIDTH), lambda i: (0, KEY_VALUE_HEADS + i // per_group))
    return pl.pallas_call(
        functools.partial(attention_kernel, heads),
        grid=(QUERY_HEADS // heads,),
        in_specs=[wide, key, value, key, value, wide],
        out_specs=wide,
        out_shape=jax.ShapeDtypeStruct(query.shape, BF16),
        compiler_params=pltpu.CompilerParams(vmem_limit_bytes=VMEM),
        cost_estimate=pl.CostEstimate(
            flops=8_000_000_000, bytes_accessed=4_000_000, transcendentals=1_000_000
        ),
        name="window_attention",
    )(query, previous, previous, key_value, key_value, gate)


def expert_kernel(x_ref, weight_ref, gate_ref, up_ref, down_ref, out_ref):
    rows = x_ref[...]
    gate = mm(rows, gate_ref[0])
    hidden = (gate / (1.0 + jnp.exp(-gate)) * mm(rows, up_ref[0])).astype(BF16)
    result = mm(hidden, down_ref[0]).astype(BF16).astype(F32)
    out_ref[...] = (result * weight_ref[...]).astype(BF16)


def expert_rows(tokens, weights, w_gate, w_up, w_down):
    count, width = tokens.shape
    hidden = w_gate.shape[2]
    tile = 512
    return pl.pallas_call(
        expert_kernel,
        grid=(count // tile,),
        in_specs=[
            pl.BlockSpec((tile, width), lambda i: (i, 0)),
            pl.BlockSpec((tile, 1), lambda i: (i, 0)),
            pl.BlockSpec((1, width, hidden), lambda i: (0, 0, 0)),
            pl.BlockSpec((1, width, hidden), lambda i: (0, 0, 0)),
            pl.BlockSpec((1, hidden, width), lambda i: (0, 0, 0)),
        ],
        out_specs=pl.BlockSpec((tile, width), lambda i: (i, 0)),
        out_shape=jax.ShapeDtypeStruct((count, width), BF16),
        compiler_params=pltpu.CompilerParams(vmem_limit_bytes=VMEM),
        cost_estimate=pl.CostEstimate(
            flops=6 * count * width * hidden,
            bytes_accessed=4 * count * width + 6 * width * hidden,
            transcendentals=count * hidden,
        ),
        name="expert_rows",
    )(tokens, weights, w_gate, w_up, w_down)


def body(
    delta_query,
    delta_key,
    delta_value,
    delta_gate,
    delta_beta,
    delta_decay,
    norm_gain,
    attention_query,
    attention_key_value,
    attention_gate,
    moe_input,
    routes,
    drop_mask,
    route_weights,
    w_gate,
    w_up,
    w_down,
):
    axes = ("seq", "ctx")
    n_ctx = lax.axis_size("ctx")
    n_dev = lax.axis_size("seq") * n_ctx
    me = lax.axis_index("seq") * n_ctx + lax.axis_index("ctx")

    tokens = lax.all_gather(moe_input[0], axes, axis=0, tiled=True)
    kept = drop_mask[0].astype(F32) * route_weights[0]
    chosen = routes[0].T[:, None, :] == jnp.arange(n_dev, dtype=jnp.int32)[None, :, None]
    table = jnp.sum(jnp.where(chosen, kept.T[:, None, :], 0.0), axis=0)
    tables = lax.all_gather(table, axes, axis=0, tiled=False)
    weights = lax.dynamic_index_in_dim(tables, me, axis=1, keepdims=False).reshape(-1, 1)

    previous = lax.ppermute(attention_key_value[0], "ctx", [(i, i + 1) for i in range(n_ctx - 1)])

    places = jnp.arange(delta_decay.shape[-1])
    earlier = places[None, :] <= places[:, None]
    cumulative = jnp.sum(jnp.where(earlier[None], delta_decay[0][:, None, :], 0.0), axis=-1)
    eff, direct, pack = delta_local(
        delta_query[0], delta_key[0], delta_value[0], delta_beta[0], cumulative
    )
    packs = lax.all_gather(pack, "ctx", axis=0, tiled=False)

    parts = expert_rows(tokens, weights, w_gate, w_up, w_down)
    moe_out = lax.psum_scatter(parts, axes, scatter_dimension=0, tiled=True)

    attn_out = window_attention(attention_query[0], previous, attention_key_value[0], attention_gate[0])
    delta_out = delta_finish(packs, eff, direct, delta_gate[0], norm_gain[None])
    return (delta_out[None], attn_out[None], moe_out[None])


def solution(mesh):
    placed = (
        P("seq", "ctx", None),
        P("seq", "ctx", None),
        P("seq", "ctx", None),
        P("seq", "ctx", None),
        P("seq", None, "ctx"),
        P("seq", None, "ctx"),
        P(),
        P("seq", "ctx", None),
        P("seq", "ctx", None),
        P("seq", "ctx", None),
        P("seq", "ctx", None),
        P("seq", "ctx", None),
        P("seq", "ctx", None),
        P("seq", "ctx", None),
        P(("seq", "ctx"), None, None),
        P(("seq", "ctx"), None, None),
        P(("seq", "ctx"), None, None),
    )
    return jax.shard_map(
        body,
        mesh=mesh,
        in_specs=placed,
        out_specs=(P("seq", "ctx", None), P("seq", "ctx", None), P("seq", "ctx", None)),
        check_vma=False,
    )
```

time: 1060 us -> 489 us (0.46)
  waiting for transfers between devices: 530 us -> 340 us
  other arithmetic: 182 us -> 1.37 us
  matrix products: 155 us -> 0 us
  local copies, waits for them, and re-layouts: 150 us -> 7.84 us
  Pallas kernels: 0 us -> 76.3 us
  blocking collectives: 0 us -> 40 us
  starting transfers between devices: 16.4 us -> 2.27 us
    all_to_all x2 -> x0, waiting for transfers between devices: 334 us -> none  [the longest x1 334 us: expert_layer(): lax.all_to_all(outgoing.reshape(n_dev, capacity, width), ('seq', 'ctx'),...]
    ppermute x1, waiting for transfers between devices: 196 us -> 14.7 us  [body(): lax.ppermute(attention_key_value[0], 'ctx', [(i, i + 1) for i in range(n_...]
    reduce_scatter x0 -> x1, waiting for transfers between devices: none -> 171 us  [body(): moe_out = lax.psum_scatter(parts, axes, scatter_dimension=0, tiled=True)]
    all_gather x2, waiting for transfers between devices: 0.01 us -> 153 us  [the longest x1 100 us: body(): packs = lax.all_gather(pack, 'ctx', axis=0, tiled=False)]
    dot_general x27 -> x0, matrix products: 151 us -> none  [the longest x8 56.5 us: compose(): jnp.einsum('hvk,hkl->hvl', earlier[1], later[0], precision=precise)]
    another operation x5 -> x0, other arithmetic: 146 us -> none  [the longest x4 145 us: span_terms(): jax.scipy.linalg.solve_triangular(system, right_side, lower=True, unit_di...]
    pallas_call x0 -> x4, Pallas kernels: none -> 76.3 us  [the longest x1 32.9 us: expert_rows(): pl.pallas_call(expert_kernel, grid=(count // tile,), in_specs=[pl.BlockSp...]
    dynamic_slice x16 -> x0, local copies, waits for them, and re-layouts: 48.9 us -> none  [lap(): new = combine(before, jax.tree.map(lambda part: part[k], everything))]
  transfers between devices with their start and end apart: 5 -> 4, of which waited for: 2 -> 4; matrix products, arithmetic and copies ran while one was open for 24% -> 0% of each run, Pallas kernels for 0% -> 16%
where the time goes in v1:
time: 489 us; the launch traced here: 481 us
  waiting for transfers between devices  340 us (70%)
  Pallas kernels  76.3 us (16%)
  blocking collectives  40 us (8%)
  between operations  13.8 us (3%)
  local copies, waits for them, and re-layouts  7.84 us (2%)
    reduce_scatter x1, waiting for transfers between devices, body(): moe_out = lax.psum_scatter(parts, axes, scatter_dimension=0, tiled=True)  171 us
    all_gather x1, waiting for transfers between devices, body(): packs = lax.all_gather(pack, 'ctx', axis=0, tiled=False)  100 us
    all_gather x1, waiting for transfers between devices, body(): tokens = lax.all_gather(moe_input[0], axes, axis=0, tiled=True)  52.8 us
    all_gather x1, blocking collectives, body(): tables = lax.all_gather(table, axes, axis=0, tiled=False)  40 us
    pallas_call x1, Pallas kernels, expert_rows(): pl.pallas_call(expert_kernel, grid=(count // tile,), in_specs=[pl.BlockSp...  32.9 us
    pallas_call x1, Pallas kernels, delta_local(): pl.pallas_call(functools.partial(delta_local_kernel, key_heads), grid=(HK...  21.2 us
    ppermute x1, waiting for transfers between devices, body(): lax.ppermute(attention_key_value[0], 'ctx', [(i, i + 1) for i in range(n_...  14.7 us
    pallas_call x1, Pallas kernels, delta_finish(): pl.pallas_call(functools.partial(delta_finish_kernel, heads), grid=(HV //...  14.4 us
  transfers between devices with their start and end apart: 4, of which 4 were waited for; matrix products, arithmetic and copies ran while one was open for 0% of the time, Pallas kernels for 16%

profile of v1, /device:TPU:18, one launch (start us, length us, event | category | flops | bytes accessed | tf_op | source)
XLA Modules:
  0.0 481.2 jit_solution(12781390481609115097)
XLA Ops:
  7.2 0.0 all-gather.8.cloned.1.call-start
  7.2 0.7 all-gather.8.cloned.1.call-update
  7.9 0.0 all-gather.6.cloned.1.call-start
  8.0 1.3 select_reduce_fusion.cum_ref
  9.3 0.0 copy-start
  9.3 1.2 copy-done
  10.5 1.0 copy-done.4
  11.6 1.0 copy-done.5
  12.6 0.7 copy-done.7
  13.3 21.2 %delta_local.1 = (f32[32,128,128]{2,1,0:T(8,128)}, f32[32,128,128]{2,1,0:T(8,128)}, bf16[32,272,128]{2,1,0:T(8,128)(2,1)}) custom-call(bf16[128,2048]{1,0:T(8,128)(2,1)S(1)} %bitcast.32, bf16[128,2048]{1,0:T(8,128)(2,1)S(1)} %bitcast.33, bf16[128,4096]{1,0:T(8,128)(2,1)S(1)} %bitcast.28, f32[32,128]{1,0:T(8,128)S(1)} %bitcast.37, ...), custom_call_target="tpu_custom_call" | custom-call | flops 60000002048 | bytes 12000000 | tf_op jit(solution)/shard_map/delta_local/pallas_call | solution.py:137
  34.5 0.0 all-gather.6.cloned.1.call-update
  34.6 0.0 reduce-scatter.2.cloned.1.call-start
  34.6 0.6 copy-done.11
  35.2 0.0 copy-done.12
  35.3 0.0 copy-done.10
  35.3 40.0 %all-gather.2 = f32[1024,128]{1,0:T(8,128)S(1)} all-gather(f32[32,128]{1,0:T(8,128)S(1)} %select_reduce_fusion.1), channel_id=4, replica_groups=mesh['seq'=4,'ctx'=8] {'seq','ctx'}, dimensions={0}, use_global_device_ids=true | all-gather | bytes 540672 | tf_op jit(solution)/shard_map/all_gather | solution.py:328
  75.3 0.6 copy.22.weight_ref
  76.0 52.8 %all-gather.8.cloned.1.call-done = bf16[1,4096,2048]{2,1,0:T(8,128)(2,1)} async-done(((bf16[1,128,2048]{2,1,0:T(8,128)(2,1)}), bf16[1,4096,2048]{2,1,0:T(8,128)(2,1)}) %all-gather.8.cloned.1.call-update) | async-done | bytes 16777232 | tf_op jit(solution)/shard_map/all_gather | solution.py:324
  128.7 32.9 %expert_rows.1 = bf16[4096,2048]{1,0:T(8,128)(2,1)} custom-call(bf16[4096,2048]{1,0:T(8,128)(2,1)} %bitcast.44, f32[4096,1]{1,0:T(8,128)S(1)} %copy.22.weight_ref, bf16[1,2048,512]{2,1,0:T(8,128)(2,1)} %gate_ref.1, bf16[1,2048,512]{2,1,0:T(8,128)(2,1)} %up_ref.1, bf16[1,512,2048]{2,1,0:T(8,128)(2,1)} %down_ref.1), custom_call_target="tpu_custom_call" | custom-call | flops 25769803776 | bytes 39845888 | tf_op jit(solution)/shard_map/expert_rows/pallas_call | solution.py:278
  161.6 0.0 reduce-scatter.2.cloned.1.call-update
  161.6 0.9 copy-done.6
  162.6 2.2 collective-permute-start
  164.7 14.7 %collective-permute-done.k_old_ref.v_old_ref = bf16[128,1024]{1,0:T(8,128)(2,1)S(1)} collective-permute-done((bf16[128,1024]{1,0:T(8,128)(2,1)S(1)}, bf16[128,1024]{1,0:T(8,128)(2,1)S(1)}, u32[]{:S(2)}, u32[]{:S(2)}) %collective-permute-start) | collective-permute-done | bytes 262176 | tf_op jit(solution)/shard_map/ppermute | solution.py:331
  179.5 0.0 copy-done.1
  179.5 0.0 copy-done.2
  179.5 7.8 %window_attention.1 = bf16[128,4096]{1,0:T(8,128)(2,1)} custom-call(bf16[128,4096]{1,0:T(8,128)(2,1)S(1)} %bitcast.29, bf16[128,1024]{1,0:T(8,128)(2,1)S(1)} %collective-permute-done.k_old_ref.v_old_ref, bf16[128,1024]{1,0:T(8,128)(2,1)S(1)} %collective-permute-done.k_old_ref.v_old_ref, bf16[128,1024]{1,0:T(8,128)(2,1)S(1)} %bitcast.35, ...), custom_call_target="tpu_custom_call" | custom-call | flops 8000000000 | bytes 4000000 | tf_op jit(solution)/shard_map/window_attention/pallas_call | solution.py:252
  187.3 100.3 %all-gather.6.cloned.1.call-done = bf16[256,272,128]{2,1,0:T(8,128)(2,1)} async-done(((bf16[32,272,128]{2,1,0:T(8,128)(2,1)}), bf16[256,272,128]{2,1,0:T(8,128)(2,1)}) %all-gather.6.cloned.1.call-update) | async-done | bytes 17825808 | tf_op jit(solution)/shard_map/all_gather | solution.py:339
  287.6 0.0 copy-done.3
  287.6 0.0 copy-done.8
  287.6 1.6 copy-done.9
  289.2 14.4 %delta_finish.1 = bf16[128,4096]{1,0:T(8,128)(2,1)} custom-call(bf16[8,32,272,128]{3,2,1,0:T(8,128)(2,1)} %bitcast.43, f32[32,128,128]{2,1,0:T(8,128)S(1)} %copy-done.9, f32[32,128,128]{2,1,0:T(8,128)} %get-tuple-element.8.direct_ref, bf16[128,4096]{1,0:T(8,128)(2,1)S(1)} %bitcast.31, f32[1,128]{1,0:T(1,128)S(1)} %bitcast.38), custom_call_target="tpu_custom_call" | custom-call | flops 20000000000 | bytes 24000000 | tf_op jit(solution)/shard_map/delta_finish/pallas_call | solution.py:204
  303.7 171.0 %reduce-scatter.2.cloned.1.call-done = bf16[128,2048]{1,0:T(8,128)(2,1)} async-done(((bf16[4096,2048]{1,0:T(8,128)(2,1)}), bf16[128,2048]{1,0:T(8,128)(2,1)}) %reduce-scatter.2.cloned.1.call-update) | async-done | bytes 524304 | tf_op jit(solution)/shard_map/reduce_scatter | solution.py:342
  (18 shorter events, 0.1 us)
Async XLA Ops:
  7.2 121.6 %all-gather.8.cloned.1.call-start = ((), (), s32[]{:S(2)}) async-start(), calls=%async_computation.3 | async-start | bytes 17301504 | tf_op jit(solution)/shard_map/all_gather | solution.py:324
  7.9 279.7 %all-gather.6.cloned.1.call-start = ((), (), s32[]{:S(2)}) async-start(), calls=%async_computation.2 | async-start | bytes 20054016 | tf_op jit(solution)/shard_map/all_gather | solution.py:339
  9.3 1.2 copy-start
  10.5 1.0 copy-start.4
  11.6 1.0 copy-start.5
  12.6 0.7 copy-start.7
  34.5 0.7 copy-start.11
  34.5 0.7 copy-start.12
  34.5 0.7 copy-start.10
  34.6 440.1 %reduce-scatter.2.cloned.1.call-start = ((), (), s32[]{:S(2)}) async-start(), calls=%async_computation.1 | async-start | bytes 17301504 | tf_op jit(solution)/shard_map/reduce_scatter | solution.py:342
  161.6 1.0 copy-start.6
  161.6 17.9 %copy-start.1 = (bf16[1,128,4096]{2,1,0:T(8,128)(2,1)S(1)}, bf16[1,128,4096]{2,1,0:T(8,128)(2,1)}, u32[]{:S(2)}) copy-start(bf16[1,128,4096]{2,1,0:T(8,128)(2,1)} %param.24) | copy-start | bytes 3145732
  161.6 17.9 %copy-start.2 = (bf16[1,128,4096]{2,1,0:T(8,128)(2,1)S(1)}, bf16[1,128,4096]{2,1,0:T(8,128)(2,1)}, u32[]{:S(2)}) copy-start(bf16[1,128,4096]{2,1,0:T(8,128)(2,1)} %param.26) | copy-start | bytes 3145732
  162.6 16.9 %collective-permute-start = (bf16[128,1024]{1,0:T(8,128)(2,1)S(1)}, bf16[128,1024]{1,0:T(8,128)(2,1)S(1)}, u32[]{:S(2)}, u32[]{:S(2)}) collective-permute-start(bf16[128,1024]{1,0:T(8,128)(2,1)S(1)} %bitcast.34), channel_id=1, source_target_pairs={{0,1},{1,2},{2,3},{3,4},{4,5},{5,6},{6,7},{8,9},{9,10},{10,11},{11... | collective-permute-start | bytes 786440 | tf_op jit(solution)/shard_map/ppermute | solution.py:331
  179.5 108.2 %copy-start.3 = (bf16[1,128,4096]{2,1,0:T(8,128)(2,1)S(1)}, bf16[1,128,4096]{2,1,0:T(8,128)(2,1)}, u32[]{:S(2)}) copy-start(bf16[1,128,4096]{2,1,0:T(8,128)(2,1)} %param.20) | copy-start | bytes 3145732
  179.5 108.2 %copy-start.8 = (f32[128]{0:T(128)S(1)}, f32[128]{0:T(128)}, u32[]{:S(2)}) copy-start(f32[128]{0:T(128)} %param.23) | copy-start | bytes 1540
  287.6 1.6 copy-start.9
Sparse Core Ops, SparseCore 0:
  11.0 117.6 all-gather.7
  130.4 157.2 all-gather.5
  290.5 184.0 reduce-scatter.1
